TPU v7x, 512 devices: a whole 4x4x16 slice. The times are simulated.
512 devices in a mesh: section: 16 (over z_lo, core), expert: 8 (over y, z_hi), dp: 4 (over x).
Axes of the slice: x: 4, y: 4, z: 16 (z_hi: 2, z_lo: 8; z = z_hi * 8 + z_lo), core: 2. Of those that a mesh axis runs over, the one named last changes fastest.
Arguments:
- tokens: bfloat16 [65536, 3072], P(('section', 'expert', 'dp')), parts along dimension 0, may hold values from -6 to 6
- expert_ids: int32 [65536, 2], P(('section', 'expert', 'dp')), parts along dimension 0, may hold values from 0 to 7, all different within a row; in each aligned block of 128 rows (0 to 127, 128 to 255, ...) at most 64 rows name the same one
- gate_scores: float32 [65536, 2], P(('section', 'expert', 'dp')), parts along dimension 0, may hold values from 0.1 to 1
- gate_weight: bfloat16 [128, 3072, 128], P(('section', 'expert'), 'dp'), parts along dimension 0, may hold values from -0.109375 to 0.109375
- up_weight: bfloat16 [128, 3072, 128], P(('section', 'expert'), 'dp'), parts along dimension 0, may hold values from -0.109375 to 0.109375
- down_weight: bfloat16 [128, 3072, 128], P(('section', 'expert'), 'dp'), parts along dimension 0, may hold values from -0.5 to 0.5
- grad_out: bfloat16 [65536, 3072], P(('section', 'expert', 'dp')), parts along dimension 0, may hold values from -6 to 6
Outputs:
- layer_out: bfloat16 [65536, 3072], P(('section', 'expert', 'dp')), parts along dimension 0
- grad_tokens: bfloat16 [65536, 3072], P(('section', 'expert', 'dp')), parts along dimension 0
- grad_scores: float32 [65536, 2], P(('section', 'expert', 'dp')), parts along dimension 0
- grad_gate_weight: float32 [128, 3072, 128], P(('section', 'expert'), 'dp'), parts along dimension 0
- grad_up_weight: float32 [128, 3072, 128], P(('section', 'expert'), 'dp'), parts along dimension 0
- grad_down_weight: float32 [128, 3072, 128], P(('section', 'expert'), 'dp'), parts along dimension 0
There are 16 independent parts, one for each index of `section`. A program takes and returns all parts, laid end to end along the dimension named above; each array names one. Nothing has to cross between parts.
Inputs may be any that keep to these rules, and one draw needn't show every extreme that they name: `expert_ids`: each token names 2 different experts. In each aligned block of 128 rows (the rows of one device) no expert is named by more than 64 rows, and in some blocks an expert is named by exactly 64 rows.
All inputs are finite; a program needn't handle non-finite values.
Results may differ from a plain program's by a relative error of at most 0.012.
Values may be sent and summed in bfloat16 or wider, within the bound.
A program may use at most 64 MiB of HBM per device.

v0:
```python
import jax
import jax.numpy as jnp
from jax import lax
from jax.sharding import PartitionSpec as P

TOP = 2


def forward_rows(received, gate_full, up_full, down_full):
    gate_pre = jnp.einsum("snd,df->snf", received, gate_full, preferred_element_type=jnp.float32)
    up_pre = jnp.einsum("snd,df->snf", received, up_full, preferred_element_type=jnp.float32)
    hidden_act = (gate_pre * jax.nn.sigmoid(gate_pre) * up_pre).astype(jnp.bfloat16)
    expert_out = jnp.einsum(
        "snf,df->snd", hidden_act, down_full, preferred_element_type=jnp.float32
    ).astype(jnp.bfloat16)
    return (expert_out, hidden_act, gate_pre, up_pre)


def backward_rows(grad_rows, gate_pre, up_pre, gate_full, up_full, down_full):
    grad_act = jnp.einsum("snd,df->snf", grad_rows, down_full, preferred_element_type=jnp.float32)
    sigmoid_gate = jax.nn.sigmoid(gate_pre)
    gate_grad = (grad_act * up_pre * sigmoid_gate * (1.0 + gate_pre * (1.0 - sigmoid_gate))).astype(
        jnp.bfloat16
    )
    up_grad = (grad_act * gate_pre * sigmoid_gate).astype(jnp.bfloat16)
    input_grad = (
        jnp.einsum("snf,df->snd", gate_grad, gate_full, preferred_element_type=jnp.float32)
        + jnp.einsum("snf,df->snd", up_grad, up_full, preferred_element_type=jnp.float32)
    ).astype(jnp.bfloat16)
    return (gate_grad, up_grad, input_grad)


def local(tokens, expert_ids, gate_scores, gate_weight, up_weight, down_weight, grad_out):
    tok_rows, model_width = tokens.shape
    experts = lax.axis_size("expert")
    capacity = min(tok_rows, tok_rows * TOP * 2 // experts)
    slot_count = tok_rows * TOP
    flat_ids = expert_ids.reshape(slot_count)
    flat_scores = gate_scores.reshape(slot_count)
    one_hot = (flat_ids[:, None] == jnp.arange(experts, dtype=jnp.int32)[None, :]).astype(jnp.int32)
    before = jnp.cumsum(one_hot, axis=0) - one_hot
    position = jnp.sum(before * one_hot, axis=1)
    slot_index = flat_ids * capacity + position
    slot_table = (
        jnp.full((experts * capacity,), slot_count, jnp.int32)
        .at[slot_index]
        .set(jnp.arange(slot_count, dtype=jnp.int32))
    )
    filled = slot_table < slot_count
    source = jnp.minimum(slot_table, slot_count - 1)
    token_of = source // TOP
    token_send = jnp.where(filled[:, None], tokens[token_of], jnp.zeros((), jnp.bfloat16))
    token_send = token_send.reshape(experts, capacity, model_width)
    scale_send = jnp.where(filled, flat_scores[source], jnp.float32(0.0))
    grad_send = (scale_send[:, None] * grad_out[token_of].astype(jnp.float32)).astype(jnp.bfloat16)
    grad_send = grad_send.reshape(experts, capacity, model_width)
    gate_all, up_all, down_all = (
        lax.all_gather(gate_weight, "dp", axis=1, tiled=True),
        lax.all_gather(up_weight, "dp", axis=1, tiled=True),
        lax.all_gather(down_weight, "dp", axis=1, tiled=True),
    )
    gate_full = gate_all[0]
    up_full = up_all[0]
    down_full = down_all[0]
    received = lax.all_to_all(token_send, "expert", split_axis=0, concat_axis=0, tiled=True)
    expert_out, expert_hidden_act, gate_pre, up_pre = forward_rows(
        received, gate_full, up_full, down_full
    )
    expert_out, hidden_act, gate_pre, up_pre, token_recv = (
        expert_out,
        expert_hidden_act,
        gate_pre,
        up_pre,
        received,
    )
    returned = lax.all_to_all(expert_out, "expert", split_axis=0, concat_axis=0, tiled=True)
    grad_recv = lax.all_to_all(grad_send, "expert", split_axis=0, concat_axis=0, tiled=True)
    gate_grad, up_grad, input_grad = backward_rows(
        grad_recv, gate_pre, up_pre, gate_full, up_full, down_full
    )
    input_back = lax.all_to_all(input_grad, "expert", split_axis=0, concat_axis=0, tiled=True)
    out_slots = returned.reshape(experts * capacity, model_width)[slot_index].reshape(
        tok_rows, TOP, model_width
    )
    input_slots = input_back.reshape(experts * capacity, model_width)[slot_index].reshape(
        tok_rows, TOP, model_width
    )
    out_float = out_slots.astype(jnp.float32)
    layer_out = jnp.sum(gate_scores[:, :, None] * out_float, axis=1).astype(jnp.bfloat16)
    grad_scores = jnp.sum(grad_out.astype(jnp.float32)[:, None, :] * out_float, axis=2)
    grad_tokens = jnp.sum(input_slots.astype(jnp.float32), axis=1).astype(jnp.bfloat16)
    gate_term = jnp.einsum("snd,snf->df", token_recv, gate_grad, preferred_element_type=jnp.float32)
    up_term = jnp.einsum("snd,snf->df", token_recv, up_grad, preferred_element_type=jnp.float32)
    down_term = jnp.einsum("snd,snf->df", grad_recv, hidden_act, preferred_element_type=jnp.float32)
    summed = lax.psum_scatter(
        jnp.concatenate([gate_term, up_term, down_term], axis=1).astype(jnp.bfloat16),
        "dp",
        scatter_dimension=0,
        tiled=True,
    ).astype(jnp.float32)
    hidden_units = gate_weight.shape[2]
    grad_gate_weight = summed[:, :hidden_units][None]
    grad_up_weight = summed[:, hidden_units : 2 * hidden_units][None]
    grad_down_weight = summed[:, 2 * hidden_units :][None]
    return (layer_out, grad_tokens, grad_scores, grad_gate_weight, grad_up_weight, grad_down_weight)


def solution(mesh):
    placed = (
        P(("section", "expert", "dp"), None),
        P(("section", "expert", "dp"), None),
        P(("section", "expert", "dp"), None),
        P(("section", "expert"), "dp", None),
        P(("section", "expert"), "dp", None),
        P(("section", "expert"), "dp", None),
        P(("section", "expert", "dp"), None),
    )
    return jax.shard_map(
        local,
        mesh=mesh,
        in_specs=placed,
        out_specs=(
            P(("section", "expert", "dp"), None),
            P(("section", "expert", "dp"), None),
            P(("section", "expert", "dp"), None),
            P(("section", "expert"), "dp", None),
            P(("section", "expert"), "dp", None),
            P(("section", "expert"), "dp", None),
        ),
        check_vma=False,
    )
```

profile of v0, /device:TPU:1, one launch (start us, length us, event | category | flops | bytes accessed | tf_op | source)
XLA Modules:
  0.0 685.4 jit_solution(15301803080129928541)
XLA Ops:
  10.2 1.4 scatter_custom_fusion
  12.6 3.5 gather_fusion.2
  16.2 3.8 gather_fusion
  20.0 3.9 broadcast_select_fusion
  23.9 18.4 %all-to-all-start = ((bf16[8,64,3072]{2,1,0:T(8,128)(2,1)}), bf16[8,64,3072]{2,1,0:T(8,128)(2,1)}, u32[]{:S(2)}, u32[]{:S(2)}) async-start(bf16[8,64,3072]{2,1,0:T(8,128)(2,1)} %broadcast_select_fusion), calls=%async_computation | async-start | bytes 6291456 | tf_op jit(solution)/shard_map/all_to_all | solution.py:65
  42.4 3.8 gather_fusion.3
  46.2 4.6 fusion
  50.8 62.9 %all-to-all-done = bf16[8,64,3072]{2,1,0:T(8,128)(2,1)} async-done(((bf16[8,64,3072]{2,1,0:T(8,128)(2,1)}), bf16[8,64,3072]{2,1,0:T(8,128)(2,1)}, u32[]{:S(2)}, u32[]{:S(2)}) %all-to-all-start) | async-done | bytes 3145760 | tf_op jit(solution)/shard_map/all_to_all | solution.py:65
  113.7 4.5 all-to-all-start.2
  118.2 12.0 %all_gather.9 = bf16[1,3072,128]{2,1,0:T(8,128)(2,1)S(1)} all-gather(bf16[1,768,128]{2,1,0:T(8,128)(2,1)S(1)} %copy-done.4), channel_id=1, replica_groups=mesh['section'=16,'expert'=8,'dp'=4] {'dp'}, dimensions={1}, use_global_device_ids=true | all-gather | bytes 983040 | tf_op jit(solution)/shard_map/all_gather | solution.py:58
  130.1 10.4 %all_gather.10 = bf16[1,3072,128]{2,1,0:T(8,128)(2,1)S(1)} all-gather(bf16[1,768,128]{2,1,0:T(8,128)(2,1)S(1)} %copy-done.5), channel_id=1, replica_groups=mesh['section'=16,'expert'=8,'dp'=4] {'dp'}, dimensions={1}, use_global_device_ids=true | all-gather | bytes 983040 | tf_op jit(solution)/shard_map/all_gather | solution.py:59
  140.6 13.3 %all_gather.11 = bf16[1,3072,128]{2,1,0:T(8,128)(2,1)} all-gather(bf16[1,768,128]{2,1,0:T(8,128)(2,1)} %param.12), channel_id=1, replica_groups=mesh['section'=16,'expert'=8,'dp'=4] {'dp'}, dimensions={1}, use_global_device_ids=true | all-gather | bytes 983040 | tf_op jit(solution)/shard_map/all_gather | solution.py:60
  153.9 3.6 fusion.12
  157.4 3.6 fusion.8
  161.0 162.7 %all-to-all-done.2 = bf16[8,64,3072]{2,1,0:T(8,128)(2,1)} async-done(((bf16[8,64,3072]{2,1,0:T(8,128)(2,1)}), bf16[8,64,3072]{2,1,0:T(8,128)(2,1)}, u32[]{:S(2)}, u32[]{:S(2)}) %all-to-all-start.2) | async-done | bytes 3145760 | tf_op jit(solution)/shard_map/all_to_all | solution.py:77
  323.7 3.8 multiply_convert_fusion
  328.5 2.7 add_convert_fusion
  331.2 12.3 %all-to-all-start.3 = ((bf16[8,64,3072]{2,1,0:T(8,128)(2,1)}), bf16[8,64,3072]{2,1,0:T(8,128)(2,1)}, u32[]{:S(2)}, u32[]{:S(2)}) async-start(bf16[8,64,3072]{2,1,0:T(8,128)(2,1)} %add_convert_fusion), calls=%async_computation.3 | async-start | bytes 6291456 | tf_op jit(solution)/shard_map/all_to_all | solution.py:81
  343.6 2.6 convolution_convert_fusion
  346.2 122.9 %all-to-all-done.3 = bf16[8,64,3072]{2,1,0:T(8,128)(2,1)} async-done(((bf16[8,64,3072]{2,1,0:T(8,128)(2,1)}), bf16[8,64,3072]{2,1,0:T(8,128)(2,1)}, u32[]{:S(2)}, u32[]{:S(2)}) %all-to-all-start.3) | async-done | bytes 3145760 | tf_op jit(solution)/shard_map/all_to_all | solution.py:81
  469.1 11.1 %all-to-all-start.1 = ((bf16[8,64,3072]{2,1,0:T(8,128)(2,1)}), bf16[8,64,3072]{2,1,0:T(8,128)(2,1)}, u32[]{:S(2)}, u32[]{:S(2)}) async-start(bf16[8,64,3072]{2,1,0:T(8,128)(2,1)} %convolution_convert_fusion), calls=%async_computation.1 | async-start | bytes 6291456 | tf_op jit(solution)/shard_map/all_to_all | solution.py:76
  480.4 2.5 fusion.3
  482.9 2.5 fusion.1
  485.4 2.5 fusion.2
  488.0 1.6 pad_maximum_fusion
  490.9 147.7 %reduce-scatter.2.cloned.1.call-done = bf16[768,384]{0,1:T(8,128)(2,1)} async-done(((bf16[3072,384]{0,1:T(8,128)(2,1)}), bf16[768,384]{0,1:T(8,128)(2,1)}) %reduce-scatter.2.cloned.1.call-update) | async-done | bytes 589840 | tf_op jit(solution)/shard_map/reduce_scatter | solution.py:95
  642.6 6.6 gather_fusion.4
  649.2 3.5 reshape.107
  652.7 6.6 gather_fusion.1
  659.3 4.8 reshape.108
  664.1 8.7 %multiply_reduce_fusion = (f32[128,2]{1,0:T(8,128)S(1)}, bf16[128,3072]{1,0:T(8,128)(2,1)}) fusion(f32[128,2,3072]{2,1,0:T(2,128)} %reshape.108, f32[128,3072]{1,0:T(8,128)} %convert_element_type.68, f32[128,2]{1,0:T(8,128)S(1)} %copy.25), kind=kLoop, calls=%fused_computation.16 | loop fusion | flops 2752256 | bytes 5507072 | tf_op jit(solution)/shard_map/reduce_sum | solution.py:90
  673.4 5.1 reduce_sum.44
  (45 shorter events, 11.3 us)
Async XLA Ops:
  7.2 9.0 %copy-start = (bf16[128,3072]{1,0:T(8,128)(2,1)S(1)}, bf16[128,3072]{1,0:T(8,128)(2,1)}, u32[]{:S(2)}) copy-start(bf16[128,3072]{1,0:T(8,128)(2,1)} %param.7) | copy-start | bytes 2359300
  23.9 18.5 %copy-start.1 = (bf16[128,3072]{1,0:T(8,128)(2,1)S(1)}, bf16[128,3072]{1,0:T(8,128)(2,1)}, u32[]{:S(2)}) copy-start(bf16[128,3072]{1,0:T(8,128)(2,1)} %param.13) | copy-start | bytes 2359300
  23.9 89.8 %all-to-all-start = ((bf16[8,64,3072]{2,1,0:T(8,128)(2,1)}), bf16[8,64,3072]{2,1,0:T(8,128)(2,1)}, u32[]{:S(2)}, u32[]{:S(2)}) async-start(bf16[8,64,3072]{2,1,0:T(8,128)(2,1)} %broadcast_select_fusion), calls=%async_computation | async-start | bytes 6291456 | tf_op jit(solution)/shard_map/all_to_all | solution.py:65
  50.8 67.4 %copy-start.4 = (bf16[1,768,128]{2,1,0:T(8,128)(2,1)S(1)}, bf16[1,768,128]{2,1,0:T(8,128)(2,1)}, u32[]{:S(2)}) copy-start(bf16[1,768,128]{2,1,0:T(8,128)(2,1)} %param.10) | copy-start | bytes 589828
  50.8 79.4 %copy-start.5 = (bf16[1,768,128]{2,1,0:T(8,128)(2,1)S(1)}, bf16[1,768,128]{2,1,0:T(8,128)(2,1)}, u32[]{:S(2)}) copy-start(bf16[1,768,128]{2,1,0:T(8,128)(2,1)} %param.11) | copy-start | bytes 589828
  113.7 210.1 %all-to-all-start.2 = ((bf16[8,64,3072]{2,1,0:T(8,128)(2,1)}), bf16[8,64,3072]{2,1,0:T(8,128)(2,1)}, u32[]{:S(2)}, u32[]{:S(2)}) async-start(bf16[8,64,3072]{2,1,0:T(8,128)(2,1)} %fusion), calls=%async_computation.2 | async-start | bytes 6291456 | tf_op jit(solution)/shard_map/all_to_all | solution.py:77
  331.2 12.3 %copy-start.2 = (bf16[1,3072,128]{2,1,0:T(8,128)(2,1)S(1)}, bf16[1,3072,128]{2,1,0:T(8,128)(2,1)}, u32[]{:S(2)}) copy-start(bf16[1,3072,128]{2,1,0:T(8,128)(2,1)} %all_gather.11) | copy-start | bytes 2359300
  331.2 12.3 %copy-start.3 = (bf16[8,64,128]{2,1,0:T(8,128)(2,1)S(1)}, bf16[8,64,128]{2,1,0:T(8,128)(2,1)}, u32[]{:S(2)}) copy-start(bf16[8,64,128]{2,1,0:T(8,128)(2,1)} %get-tuple-element.33) | copy-start | bytes 393220
  331.2 137.8 %all-to-all-start.3 = ((bf16[8,64,3072]{2,1,0:T(8,128)(2,1)}), bf16[8,64,3072]{2,1,0:T(8,128)(2,1)}, u32[]{:S(2)}, u32[]{:S(2)}) async-start(bf16[8,64,3072]{2,1,0:T(8,128)(2,1)} %add_convert_fusion), calls=%async_computation.3 | async-start | bytes 6291456 | tf_op jit(solution)/shard_map/all_to_all | solution.py:81
  469.1 183.6 %all-to-all-start.1 = ((bf16[8,64,3072]{2,1,0:T(8,128)(2,1)}), bf16[8,64,3072]{2,1,0:T(8,128)(2,1)}, u32[]{:S(2)}, u32[]{:S(2)}) async-start(bf16[8,64,3072]{2,1,0:T(8,128)(2,1)} %convolution_convert_fusion), calls=%async_computation.1 | async-start | bytes 6291456 | tf_op jit(solution)/shard_map/all_to_all | solution.py:76
  480.2 158.4 %reduce-scatter.2.cloned.1.call-start = ((), (), s32[]{:S(2)}) async-start(), calls=%async_computation.5 | async-start | bytes 2949120 | tf_op jit(solution)/shard_map/reduce_scatter | solution.py:95
Sparse Core Ops, SparseCore 0:
  489.7 148.8 reduce-scatter.1
where the time goes:
time: 686 us; the launch traced here: 685 us
  waiting for transfers between devices  496 us (72%)
  starting transfers between devices  46.5 us (7%)
  local copies, waits for them, and re-layouts  40.2 us (6%)
  blocking collectives  35.7 us (5%)
  other arithmetic  27.7 us (4%)
  matrix products  24.8 us (4%)
  between operations  14.2 us (2%)
    all_to_all x1, waiting for transfers between devices, local(): lax.all_to_all(grad_send, 'expert', split_axis=0, concat_axis=0, tiled=True)  163 us
    reduce_scatter x1, waiting for transfers between devices, local(): lax.psum_scatter(jnp.concatenate([gate_term, up_term, down_term], axis=1)...  148 us
    all_to_all x1, waiting for transfers between devices, local(): lax.all_to_all(input_grad, 'expert', split_axis=0, concat_axis=0, tiled=T...  123 us
    all_to_all x1, waiting for transfers between devices, local(): lax.all_to_all(token_send, 'expert', split_axis=0, concat_axis=0, tiled=T...  62.9 us
    all_to_all x1, starting transfers between devices, local(): lax.all_to_all(token_send, 'expert', split_axis=0, concat_axis=0, tiled=T...  18.4 us
  transfers between devices with their start and end apart: 5, of which 4 were waited for; matrix products, arithmetic and copies ran while one was open for 6% of the time, Pallas kernels for 0%

commit v1 on v0

v1 whole, which is shorter than its diff:
```python
import functools

import jax
import jax.numpy as jnp
from jax import lax
from jax.experimental import pallas as pl
from jax.experimental.pallas import tpu as pltpu
from jax.sharding import PartitionSpec as P

MESH = pl.DeviceIdType.MESH
F32 = jnp.float32
BF16 = jnp.bfloat16
NY = 4
NX = 4
N_COPIES = 96


def dot(a, b):
    return jnp.dot(a, b, preferred_element_type=F32)


def dot_t(a, b):
    return lax.dot_general(a, b, (((1,), (1,)), ((), ())), preferred_element_type=F32)


def kernel(
    tok, go, ids, scores, wg, wu, wd,
    lo, gt, gs, dg, du, dd,
    tokb, gob, sb, wb, tok_t, go_t, gub, hsb, gsb,
    dwb, dwr, zsend, zrecv, lop, gtp, lor, gtr, gsr,
    send, recv, local_sem,
):
    rows, width = tok.shape
    part = wg.shape[0]
    hidden = wg.shape[1]
    sec, ei, x = lax.axis_index("section"), lax.axis_index("expert"), lax.axis_index("dp")
    y, zh = ei // 2, ei % 2
    other = y * 2 + 1 - zh
    z_peer = (sec, other, x)

    def y_peer(d):
        return (sec, ((y + d) % NY) * 2 + zh, x)

    def x_peer(d):
        return (sec, ei, (x + d) % NX)

    peers = [z_peer] + [y_peer(d) for d in (1, 2, 3)] + [x_peer(d) for d in (1, 2, 3)]
    barrier = pltpu.get_barrier_semaphore()
    for p in peers:
        pl.semaphore_signal(barrier, inc=1, device_id=p, device_id_type=MESH)

    count = [0]

    def copy(src, dst, to):
        k = count[0]
        count[0] = k + 1
        return pltpu.make_async_remote_copy(
            src_ref=src, dst_ref=dst, send_sem=send.at[k], recv_sem=recv.at[k],
            device_id=to, device_id_type=MESH,
        )

    lane = lax.broadcasted_iota(jnp.int32, (rows, hidden), 1)

    def x_rows(d):
        return pl.ds(pl.multiple_of(((x + d) % NX) * part, part), part)

    def slot(j):
        return pl.ds(j * rows, rows)

    mine = x_rows(0)
    w_in = (wg, wu, wd)
    own = [pltpu.make_async_copy(tok, tokb.at[slot(0)], local_sem.at[0]),
           pltpu.make_async_copy(go, gob.at[slot(0)], local_sem.at[1])]
    own += [pltpu.make_async_copy(w_in[i], wb.at[0, i, mine], local_sem.at[2 + i]) for i in range(3)]
    for c in own:
        c.start()
    table = jnp.zeros((rows, hidden), F32)
    for k in range(ids.shape[1]):
        table += jnp.where(lane == ids[:, k : k + 1], scores[:, k : k + 1], 0.0)
    sb[0] = table

    pl.semaphore_wait(barrier, len(peers))

    z_w = [copy(w_in[i], wb.at[1, i, mine], z_peer) for i in range(3)]
    y_s = [copy(sb.at[0], sb.at[NY - d], y_peer(d)) for d in (2, 1, 3)]
    y_tok = [copy(tok, tokb.at[slot(NY - d)], y_peer(d)) for d in (2, 1, 3)]
    y_go = [copy(go, gob.at[slot(NY - d)], y_peer(d)) for d in (2, 1, 3)]
    x_w = [copy(w_in[i], wb.at[0, i, mine], x_peer(d)) for i in range(3) for d in (2, 1, 3)]
    for c in z_w + y_s + x_w + y_tok + y_go:
        c.start()

    x_r = []
    for i in range(3):
        z_w[i].wait_recv()
        for d in (2, 1, 3):
            c = copy(wb.at[1, i, mine], wb.at[1, i, mine], x_peer(d))
            c.start()
            x_r.append(c)

    for c in own:
        c.wait()
    for c in y_s + y_tok + y_go:
        c.wait_recv()

    def flip(j, _):
        r = pl.ds(pl.multiple_of(j * rows, rows), rows)
        for s in range(NX):
            cols = pl.ds(s * part, part)
            tok_t[cols, r] = tokb[r, cols].T
            go_t[cols, r] = gob[r, cols].T
        return 0

    for j in range(NY):
        flip(j, 0)

    block = 2 * rows

    def hidden_rows(r, e):
        def step(m, _):
            at = pl.ds(pl.multiple_of(m * block, block), block)
            pre = jnp.zeros((block, 2 * hidden), F32)
            act = jnp.zeros((block, hidden), F32)
            for s in range(NX):
                cols = pl.ds(s * part, part)
                pre += dot(tokb[at, cols], jnp.concatenate([wb[r, 0, cols], wb[r, 1, cols]], axis=1))
                act += dot(gob[at, cols], wb[r, 2, cols])
            g, u = pre[:, :hidden], pre[:, hidden:]
            sc = jnp.concatenate([sb[2 * m], sb[2 * m + 1]], axis=0)
            big = lax.broadcasted_iota(jnp.int32, (block, hidden), 1)
            sc = jnp.sum(jnp.where(big == e, sc, 0.0), axis=1, keepdims=True)
            sig = jax.nn.sigmoid(g)
            silu = g * sig
            h = silu * u
            ga = sc * act
            hsb[r, at] = (sc * h).astype(BF16)
            gub[r, at, :hidden] = (ga * u * sig * (1.0 + g * (1.0 - sig))).astype(BF16)
            gub[r, at, hidden:] = (ga * silu).astype(BF16)
            score = jnp.sum(h * act, axis=1, keepdims=True)
            score = jnp.where(big == e, score, 0.0)
            for n in range(2):
                piece = score[n * rows : (n + 1) * rows]
                if r == 1:
                    gsb[2 * m + n] = piece
                else:
                    gsb[2 * m + n] += piece
            return 0

        lax.fori_loop(0, NY // 2, step, 0)

    def weight_grads(r, d):
        at = x_rows(d)
        both = dot(tok_t[at], gub[r]).astype(BF16)
        dwb[r, 0, at] = both[:, :hidden]
        dwb[r, 1, at] = both[:, hidden:]
        dwb[r, 2, at] = dot(go_t[at], hsb[r]).astype(BF16)
        if d == 0:
            return []
        cs = []
        for i in range(3):
            c = copy(dwb.at[r, i, at], dwr.at[r, NX - d - 1, i], x_peer(d))
            c.start()
            cs.append(c)
        return cs

    def outputs(j):
        at = slot(j)
        h = jnp.concatenate([hsb[0, at], hsb[1, at]], axis=1)
        g0, g1 = gub[0, at], gub[1, at]

        def step(s, _):
            cols = pl.ds(pl.multiple_of(s * part, part), part)
            down = jnp.concatenate([wb[0, 2, cols], wb[1, 2, cols]], axis=1)
            lop[at, cols] = dot_t(h, down).astype(BF16)
            back = dot_t(g0, jnp.concatenate([wb[0, 0, cols], wb[0, 1, cols]], axis=1))
            back += dot_t(g1, jnp.concatenate([wb[1, 0, cols], wb[1, 1, cols]], axis=1))
            gtp[at, cols] = back.astype(BF16)
            return 0

        lax.fori_loop(0, NX, step, 0)
        if j == 0:
            return []
        cs = [copy(gsb.at[j], gsr.at[NY - j - 1], y_peer(j)),
              copy(lop.at[at], lor.at[NY - j - 1], y_peer(j)),
              copy(gtp.at[at], gtr.at[NY - j - 1], y_peer(j))]
        for c in cs:
            c.start()
        return cs

    def summed(r, i):
        total = dwb[r, i, mine].astype(F32)
        for n in range(NX - 1):
            total += dwr[r, n, i].astype(F32)
        return total

    for c in x_r:
        c.wait_recv()
    hidden_rows(1, other)
    x_d1 = []
    for d in (2, 1, 3, 0):
        x_d1 += weight_grads(1, d)
    for c in x_w:
        c.wait_recv()
    hidden_rows(0, ei)
    z_d = []
    y_o = []
    for i, j in enumerate((2, 1, 3)):
        for c in x_d1[i::3]:
            c.wait_recv()
        zsend[i] = summed(1, i).astype(BF16)
        c = copy(zsend.at[i], zrecv.at[i], z_peer)
        c.start()
        z_d.append(c)
        y_o += outputs(j)
    x_d0 = []
    for d in (2, 1, 3, 0):
        x_d0 += weight_grads(0, d)
    outputs(0)

    for c in x_d0:
        c.wait_recv()
    for c in y_o:
        c.wait_recv()
    lo_sum, gt_sum, gs_sum = lop[slot(0)].astype(F32), gtp[slot(0)].astype(F32), gsb[0]
    for n in range(NY - 1):
        lo_sum += lor[n].astype(F32)
        gt_sum += gtr[n].astype(F32)
        gs_sum += gsr[n]
    lo[...] = lo_sum.astype(BF16)
    gt[...] = gt_sum.astype(BF16)
    for k in range(ids.shape[1]):
        gs[:, k : k + 1] = jnp.sum(jnp.where(lane == ids[:, k : k + 1], gs_sum, 0.0), axis=1, keepdims=True)
    for i, out in enumerate((dg, du, dd)):
        z_d[i].wait_recv()
        out[...] = summed(0, i) + zrecv[i].astype(F32)
    for c in z_w + y_s + y_tok + y_go + x_w + x_r + x_d1 + z_d + y_o + x_d0:
        c.wait_send()


def local(tokens, expert_ids, gate_scores, gate_weight, up_weight, down_weight, grad_out):
    rows, width = tokens.shape
    _, part, hidden = gate_weight.shape
    top = expert_ids.shape[1]
    vmem, hbm = pl.BlockSpec(memory_space=pltpu.VMEM), pl.BlockSpec(memory_space=pl.ANY)
    shape = jax.ShapeDtypeStruct
    scratch = [
        pltpu.VMEM((NY * rows, width), BF16),
        pltpu.VMEM((NY * rows, width), BF16),
        pltpu.VMEM((NY, rows, hidden), F32),
        pltpu.VMEM((2, 3, width, hidden), BF16),
        pltpu.VMEM((width, NY * rows), BF16),
        pltpu.VMEM((width, NY * rows), BF16),
        pltpu.VMEM((2, NY * rows, 2 * hidden), BF16),
        pltpu.VMEM((2, NY * rows, hidden), BF16),
        pltpu.VMEM((NY, rows, hidden), F32),
        pltpu.VMEM((2, 3, width, hidden), BF16),
        pltpu.VMEM((2, NX - 1, 3, part, hidden), BF16),
        pltpu.VMEM((3, part, hidden), BF16),
        pltpu.VMEM((3, part, hidden), BF16),
        pltpu.VMEM((NY * rows, width), BF16),
        pltpu.VMEM((NY * rows, width), BF16),
        pltpu.VMEM((NY - 1, rows, width), BF16),
        pltpu.VMEM((NY - 1, rows, width), BF16),
        pltpu.VMEM((NY - 1, rows, hidden), F32),
        pltpu.SemaphoreType.DMA((N_COPIES,)),
        pltpu.SemaphoreType.DMA((N_COPIES,)),
        pltpu.SemaphoreType.DMA((5,)),
    ]
    lo, gt, gs, dg, du, dd = pl.pallas_call(
        kernel,
        out_shape=[
            shape((rows, width), BF16),
            shape((rows, width), BF16),
            shape((rows, top), F32),
            shape((part, hidden), F32),
            shape((part, hidden), F32),
            shape((part, hidden), F32),
        ],
        in_specs=[hbm, hbm, vmem, vmem, hbm, hbm, hbm],
        out_specs=[vmem] * 6,
        scratch_shapes=scratch,
        compiler_params=pltpu.CompilerParams(
            collective_id=0, has_side_effects=True, vmem_limit_bytes=60 << 20
        ),
    )(tokens, grad_out, expert_ids, gate_scores, gate_weight[0], up_weight[0], down_weight[0])
    return lo, gt, gs, dg[None], du[None], dd[None]


def solution(mesh):
    rows_p = P(("section", "expert", "dp"), None)
    weight_p = P(("section", "expert"), "dp", None)
    return jax.shard_map(
        local,
        mesh=mesh,
        in_specs=(rows_p, rows_p, rows_p, weight_p, weight_p, weight_p, rows_p),
        out_specs=(rows_p, rows_p, rows_p, weight_p, weight_p, weight_p),
        check_vma=False,
    )
```

time: 686 us -> 206 us (0.30)
  waiting for transfers between devices: 496 us -> 0 us
  Pallas kernels: 0 us -> 195 us
  starting transfers between devices: 46.5 us -> 0 us
  blocking collectives: 35.7 us -> 0 us
  local copies, waits for them, and re-layouts: 40.2 us -> 10 us
  other arithmetic: 27.7 us -> 0 us
  matrix products: 24.8 us -> 0 us
  between operations: 14.2 us -> 0.66 us
    all_to_all x4 -> x0, waiting for transfers between devices: 349 us -> none  [the longest x1 163 us: local(): lax.all_to_all(grad_send, 'expert', split_axis=0, concat_axis=0, tiled=True)]
    pallas_call x0 -> x1, Pallas kernels: none -> 195 us  [local(): pl.pallas_call(kernel, out_shape=[shape((rows, width), BF16), shape((rows...]
    reduce_scatter x1 -> x0, waiting for transfers between devices: 148 us -> none  [local(): lax.psum_scatter(jnp.concatenate([gate_term, up_term, down_term], axis=1)...]
    all_to_all x4 -> x0, starting transfers between devices: 46.3 us -> none  [the longest x1 18.4 us: local(): lax.all_to_all(token_send, 'expert', split_axis=0, concat_axis=0, tiled=T...]
    all_gather x3 -> x0, blocking collectives: 35.7 us -> none  [the longest x1 13.3 us: local(): lax.all_gather(down_weight, 'dp', axis=1, tiled=True)]
    dot_general x9 -> x0, matrix products: 24.8 us -> none  [the longest x1 3.81 us: backward_rows(): jnp.einsum('snd,df->snf', grad_rows, down_full, preferred_element_type=jn...]
    gather x5 -> x0, local copies, waits for them, and re-layouts: 24.3 us -> none  [the longest x1 6.6 us: local(): input_back.reshape(experts * capacity, model_width)[slot_index]]
    reduce_sum x3 -> x0, other arithmetic: 13.9 us -> none  [the longest x1 8.68 us: local(): jnp.sum(grad_out.astype(jnp.float32)[:, None, :] * out_float, axis=2)]
  transfers between devices with their start and end apart: 5 -> 0, of which waited for: 4 -> 0; matrix products, arithmetic and copies ran while one was open for 6% -> 0% of each run, Pallas kernels for 0% -> 0%
where the time goes in v1:
time: 206 us; the launch traced here: 205 us
  Pallas kernels  195 us (95%)
  local copies, waits for them, and re-layouts  10 us (5%)
    pallas_call x1, Pallas kernels, local(): pl.pallas_call(kernel, out_shape=[shape((rows, width), BF16), shape((rows...  195 us
    unnamed x20, local copies, waits for them, and re-layouts  10 us

profile of v1, /device:TPU:1, one launch (start us, length us, event | category | flops | bytes accessed | tf_op | source)
XLA Modules:
  0.0 205.4 jit_solution(5431660678524109144)
XLA Ops:
  0.6 0.0 copy-start.4
  0.6 0.7 copy-done.4
  1.3 0.0 copy-start.5
  1.3 0.7 copy.13.ids
  2.1 0.0 copy-done.5
  2.1 0.7 copy.14.scores
  2.8 194.7 %shard_map.118 = (bf16[128,3072]{1,0:T(8,128)(2,1)}, bf16[128,3072]{1,0:T(8,128)(2,1)}, f32[128,2]{1,0:T(8,128)}, f32[768,128]{1,0:T(8,128)}, f32[768,128]{1,0:T(8,128)}, /*index=5*/f32[768,128]{1,0:T(8,128)}) custom-call(bf16[128,3072]{1,0:T(8,128)(2,1)} %tok.1, bf16[128,3072]{1,0:T(8,128)(2,1)} %go.1, s32[128,2]{1,0:T(8,128)} %copy.13.ids, ...), custom_call_target="tpu_custom_call" | custom-call | tf_op jit(solution)/shard_map/pallas_call | solution.py:268
  197.5 1.5 copy.15
  199.0 0.0 copy-start
  199.0 2.1 %copy.21 = bf16[128,3072]{1,0:T(8,128)(2,1)} copy(bf16[128,3072]{1,0:T(8,128)(2,1)} %get-tuple-element.30) | data formatting | bytes 1572864
  201.1 0.0 copy-done
  201.1 0.0 copy-start.3
  201.1 0.9 copy.22
  202.0 0.4 copy-done.3
  202.4 0.0 copy-start.2
  202.4 0.7 copy.23
  203.1 0.4 copy-done.2
  203.5 0.0 copy-start.1
  203.5 0.7 copy.24
  204.3 0.4 copy-done.1
  204.7 0.7 copy.25
Async XLA Ops:
  0.6 0.7 copy-start.4
  1.3 0.7 copy-start.5
  199.0 2.1 %copy-start = (bf16[128,3072]{1,0:T(8,128)(2,1)S(1)}, bf16[128,3072]{1,0:T(8,128)(2,1)}, u32[]{:S(2)}) copy-start(bf16[128,3072]{1,0:T(8,128)(2,1)} %get-tuple-element.31) | copy-start | bytes 2359300
  201.1 1.2 copy-start.3
  202.4 1.1 copy-start.2
  203.5 1.1 copy-start.1

commit v2 on v1

v2 whole, which is shorter than its diff:
```python
import jax
import jax.numpy as jnp
from jax import lax
from jax.experimental import pallas as pl
from jax.experimental.pallas import tpu as pltpu
from jax.sharding import PartitionSpec as P

MESH = pl.DeviceIdType.MESH
F32 = jnp.float32
BF16 = jnp.bfloat16
NY = 4
NX = 4
N_COPIES = 128


def dot(a, b):
    return jnp.dot(a, b, preferred_element_type=F32)


def dot_t(a, b):
    return lax.dot_general(a, b, (((1,), (1,)), ((), ())), preferred_element_type=F32)


def dot_l(a, b):
    return lax.dot_general(a, b, (((0,), (0,)), ((), ())), preferred_element_type=F32)


def swap(a):
    return pltpu.roll(a.astype(F32), a.shape[1] // 2, axis=1)


def low(shape):
    return lax.broadcasted_iota(jnp.int32, shape, 1) < shape[1] // 2


def kernel(
    tok, go, ids, scores, wg, wu, wd,
    lo, gt, gs, dg, du, dd,
    tokb, gob, tab, sbc, wb, pk, rw, rd, rdn,
    pre, act, act2, gub, hsb, hdup, guh, gst, gsr,
    dwb, dwr, dwq, dwqr, zsend, zrecv, lop, gtp, far, lor, gtr, dout,
    send, recv, local_sem, out_sem,
):
    rows, width = tok.shape
    part, hidden = wg.shape
    half, hp = rows // 2, part // 2
    sec, ei, x = lax.axis_index("section"), lax.axis_index("expert"), lax.axis_index("dp")
    y, zh = ei // 2, ei % 2
    other = y * 2 + 1 - zh
    z_peer = (sec, other, x)

    def y_peer(d):
        return (sec, ((y + d) % NY) * 2 + zh, x)

    def x_peer(d):
        return (sec, ei, (x + d) % NX)

    peers = [z_peer] + [y_peer(d) for d in (1, 2, 3)] + [x_peer(d) for d in (1, 2, 3)]
    barrier = pltpu.get_barrier_semaphore()
    for p in peers:
        pl.semaphore_signal(barrier, inc=1, device_id=p, device_id_type=MESH)

    made = []

    def copy(src, dst, to):
        k = len(made)
        c = pltpu.make_async_remote_copy(
            src_ref=src, dst_ref=dst, send_sem=send.at[k], recv_sem=recv.at[k],
            device_id=to, device_id_type=MESH,
        )
        made.append(c)
        c.start()
        return c

    def x_rows(d, size):
        return pl.ds(pl.multiple_of(((x + d) % NX) * size, size), size)

    def slot(j):
        return pl.ds(j * rows, rows)

    mine, mine_d = x_rows(0, part), x_rows(0, hp)
    w_in = (wg, wu, wd)
    own_w = [pltpu.make_async_copy(w_in[i], wb.at[i, mine], local_sem.at[i]) for i in range(3)]
    own_t = [pltpu.make_async_copy(tok, tokb.at[slot(0)], local_sem.at[3]),
             pltpu.make_async_copy(go, gob.at[slot(0)], local_sem.at[4])]
    for c in own_w + own_t:
        c.start()

    sub = lax.broadcasted_iota(jnp.int32, tab.shape[1:], 0)
    table = jnp.zeros(sub.shape, F32)
    for k in range(ids.shape[0]):
        table += jnp.where(sub == ids[k : k + 1], scores[k : k + 1], 0.0)
    tab[0] = table

    for c in own_w:
        c.wait()
    g, u, d = wb[0, mine].astype(F32), wb[1, mine].astype(F32), wb[2, mine].astype(F32)
    lw, ld = low((part, hidden)), low((hp, hidden))
    for h in range(2):
        if h == 0:
            gu = jnp.where(lw, g, swap(u)).astype(BF16)
            dn = jnp.where(ld, d[:hp], swap(d[hp:])).astype(BF16)
        else:
            gu = jnp.where(lw, swap(g), u).astype(BF16)
            dn = jnp.where(ld, swap(d[:hp]), d[hp:]).astype(BF16)
        pk[h, 0], pk[h, 1], pk[h, 2] = gu[:hp], gu[hp:], dn

    pl.semaphore_wait(barrier, len(peers))

    def unit(h, c):
        if c == 2:
            return rd.at[h, mine_d]
        return rw.at[h, pl.ds(pl.multiple_of(x * part + c * hp, hp), hp)]

    units = [(h, c) for h in range(2) for c in range(3)]
    z_w = [copy(pk.at[h, c], unit(h, c), z_peer) for h, c in units]
    y_s = [copy(tab.at[0], tab.at[NY - d], y_peer(d)) for d in (2, 1, 3)]
    bufs = ((tok, tokb), (go, gob))
    y_a, y_b = [], []
    for first in (True, False):
        for src, dst in bufs:
            for d in (1, 3):
                r0 = 0 if (d == 1) == first else half
                c = copy(src.at[pl.ds(r0, half)], dst.at[pl.ds((NY - d) * rows + r0, half)], y_peer(d))
                (y_a if first else y_b).append(c)
    x_w = [copy(w_in[i], wb.at[i, mine], x_peer(d)) for i in range(3) for d in (2, 1, 3)]

    y_c = []
    for n, (_, dst) in enumerate(bufs):
        for m, d in enumerate((1, 3)):
            y_a[2 * n + m].wait_recv()
            r0 = 0 if d == 1 else half
            c = copy(dst.at[pl.ds((NY - d) * rows + r0, half)], dst.at[pl.ds(2 * rows + r0, half)], y_peer(d))
            y_c.append(c)

    x_r = [[], []]

    def pass_on(n):
        h, c = units[n]
        z_w[n].wait_recv()
        for d in (2, 1, 3):
            x_r[h].append(copy(unit(h, c), unit(h, c), x_peer(d)))

    pass_on(0)
    for c in y_s:
        c.wait_recv()
    for r, e in ((0, ei), (1, other)):
        for j in range(NY):
            row = jnp.sum(jnp.where(sub == e, tab[j], 0.0), axis=0, keepdims=True)
            sbc[r, slot(j)] = jnp.broadcast_to(row, (rows, hidden)).T
    for n in (1, 2, 3):
        pass_on(n)
    for c in own_t:
        c.wait()
    for c in y_b + y_c:
        c.wait_recv()

    def add_score(j, e, col):
        flat = jnp.broadcast_to(col, (rows, hidden)).T[: sub.shape[0]]
        gst[j] += jnp.where(sub == e, flat, 0.0)

    for j in range(NY):
        gst[j] = jnp.zeros(sub.shape, F32)

    def hidden_own():
        pre[...] = dot(tokb[...], jnp.concatenate([wb[0], wb[1]], axis=1))
        act[...] = dot(gob[...], wb[2])

        def step(j, _):
            at = pl.ds(pl.multiple_of(j * rows, rows), rows)
            g, u, a, s = pre[at, :hidden], pre[at, hidden:], act[at], sbc[0, at]
            sig = jax.nn.sigmoid(g)
            silu = g * sig
            h = silu * u
            ga = s * a
            hsb[0, at] = (s * h).astype(BF16)
            gub[0, at, :hidden] = (ga * u * sig * (1.0 + g * (1.0 - sig))).astype(BF16)
            gub[0, at, hidden:] = (ga * silu).astype(BF16)
            add_score(j, ei, jnp.sum(h * a, axis=1, keepdims=True))
            return 0

        lax.fori_loop(0, NY, step, 0)

    lr = low((rows, hidden))

    def hidden_other(h):
        pre[:, :hidden] = dot(tokb[...], rw[h])
        for s in range(NX):
            dn = rd[h, pl.ds(s * hp, hp)]
            a1 = dot(gob[:, pl.ds(s * part, hp)], dn)
            a2 = dot(gob[:, pl.ds(s * part + hp, hp)], dn)
            if s == 0:
                act[...], act2[...] = a1, a2
            else:
                act[...] += a1
                act2[...] += a2

        def step(j, _):
            at = pl.ds(pl.multiple_of(j * rows, rows), rows)
            p, s = pre[at, :hidden], sbc[1, at]
            q = swap(p)
            g, u = jnp.where(lr, p, q), jnp.where(lr, q, p)
            a = act[at] + swap(act2[at])
            a = jnp.where(lr, a, swap(a))
            sig = jax.nn.sigmoid(g)
            silu = g * sig
            hid = silu * u
            ga = s * a
            hs = (s * hid).astype(BF16)
            hdup[h, at] = hs
            gu = jnp.where(lr, ga * u * sig * (1.0 + g * (1.0 - sig)), ga * silu)
            guh[h, at] = gu.astype(BF16)
            gub[1, at, h * hidden : (h + 1) * hidden] = gu.astype(BF16)
            add_score(j, other, jnp.sum(jnp.where(lr, hid * a, 0.0), axis=1, keepdims=True))
            return 0

        lax.fori_loop(0, NY, step, 0)

    def grads_other(h):
        cs = [[], [], []]
        for d in (2, 1, 3, 0):
            at = x_rows(d, part)
            gu = dot_l(tokb[:, at], guh[h]).astype(BF16)
            dn = dot_l(gob[:, at], hdup[h])
            dwq[h, d, 0], dwq[h, d, 1] = gu[:hp], gu[hp:]
            dwq[h, d, 2] = jnp.where(ld, dn[:hp], dn[hp:]).astype(BF16)
            if d:
                for c in range(3):
                    cs[c].append(copy(dwq.at[h, d, c], dwqr.at[h, NX - d - 1, c], x_peer(d)))
        return cs

    def send_z(h, c, arrivals):
        for a in arrivals:
            a.wait_recv()
        total = dwq[h, 0, c].astype(F32)
        for n in range(NX - 1):
            total += dwqr[h, n, c].astype(F32)
        zsend[h, c] = total.astype(BF16)
        return copy(zsend.at[h, c], zrecv.at[h, c], z_peer)

    for c in x_r[0]:
        c.wait_recv()
    hidden_other(0)
    x_d1 = [grads_other(0), None]
    pass_on(4)
    for c in x_w:
        c.wait_recv()
    hidden_own()
    z_d = [send_z(0, 0, x_d1[0][0])]
    pass_on(5)
    for c in (1, 2):
        z_d.append(send_z(0, c, x_d1[0][c]))

    for c in x_r[1]:
        c.wait_recv()
    hidden_other(1)
    lall = low((hp, hidden))
    for s in range(NX):
        d0, d1 = rd[0, pl.ds(s * hp, hp)].astype(F32), rd[1, pl.ds(s * hp, hp)].astype(F32)
        rdn[pl.ds(s * part, hp)] = jnp.where(lall, d0, swap(d1)).astype(BF16)
        rdn[pl.ds(s * part + hp, hp)] = jnp.where(lall, swap(d0), d1).astype(BF16)
    lfull = low((NY * rows, hidden))
    hsb[1] = jnp.where(lfull, hdup[0].astype(F32), hdup[1].astype(F32)).astype(BF16)

    hs = jnp.concatenate([hsb[0], hsb[1]], axis=1)
    gu = jnp.concatenate([gub[0], gub[1]], axis=1)
    y_far = []
    for s in range(NX):
        cols = pl.ds(s * part, part)
        lop[:, cols] = dot_t(hs, jnp.concatenate([wb[2, cols], rdn[cols]], axis=1)).astype(BF16)
        both = jnp.concatenate([wb[0, cols], wb[1, cols], rw[0, cols], rw[1, cols]], axis=1)
        gtp[:, cols] = dot_t(gu, both).astype(BF16)
        for n, buf in enumerate((lop, gtp)):
            for m, d in enumerate((1, 3)):
                r0 = m * half
                c = copy(buf.at[pl.ds(2 * rows + r0, half), cols], far.at[n, m, :, cols], y_peer(d))
                y_far.append(c)
    y_g = [copy(gst.at[d], gsr.at[NY - d - 1], y_peer(d)) for d in (2, 1, 3)]
    y_o = []
    for buf, dst in ((lop, lor), (gtp, gtr)):
        for m, d in enumerate((1, 3)):
            r0 = half - m * half
            y_o.append(copy(buf.at[pl.ds(d * rows + r0, half)], dst.at[m, pl.ds(r0, half)], y_peer(d)))
    x_d1[1] = grads_other(1)
    k = 0
    for s in range(NX):
        cols = pl.ds(s * part, part)
        for n, (buf, dst) in enumerate(((lop, lor), (gtp, gtr))):
            for m, d in enumerate((1, 3)):
                r0 = m * half
                y_far[k].wait_recv()
                k += 1
                at = pl.ds(d * rows + r0, half)
                buf[at, cols] = (buf[at, cols].astype(F32) + far[n, m, :, cols].astype(F32)).astype(BF16)
                y_o.append(copy(buf.at[at, cols], dst.at[m, pl.ds(r0, half), cols], y_peer(d)))
        if s < 3:
            z_d.append(send_z(1, s, x_d1[1][s]))

    x_d0 = []
    for d in (2, 1, 3, 0):
        at = x_rows(d, part)
        both = dot_l(tokb[:, at], gub[0]).astype(BF16)
        dwb[d, 0], dwb[d, 1] = both[:, :hidden], both[:, hidden:]
        dwb[d, 2] = dot_l(gob[:, at], hsb[0]).astype(BF16)
        if d:
            for i in range(3):
                x_d0.append(copy(dwb.at[d, i], dwr.at[NX - d - 1, i], x_peer(d)))
    for c in x_d0:
        c.wait_recv()
    for i in range(3):
        total = dwb[0, i].astype(F32)
        for n in range(NX - 1):
            total += dwr[n, i].astype(F32)
        dout[i] = total

    outs = []
    for c in y_g + y_o:
        c.wait_recv()
    for n, (buf, got, out) in enumerate(((lop, lor, lo), (gtp, gtr, gt))):
        total = buf[slot(0)].astype(F32) + got[0].astype(F32) + got[1].astype(F32)
        buf[slot(0)] = total.astype(BF16)
        c = pltpu.make_async_copy(buf.at[slot(0)], out, out_sem.at[n])
        c.start()
        outs.append(c)
    gs_sum = gst[0] + gsr[0] + gsr[1] + gsr[2]
    for k in range(ids.shape[0]):
        gs[k : k + 1] = jnp.sum(jnp.where(sub == ids[k : k + 1], gs_sum, 0.0), axis=0, keepdims=True)

    for c in z_d:
        c.wait_recv()
    for c in range(2):
        at = pl.ds(c * hp, hp)
        p1, p2 = zrecv[0, c].astype(F32), zrecv[1, c].astype(F32)
        dout[0, at] += jnp.where(ld, p1, swap(p2))
        dout[1, at] += jnp.where(ld, swap(p1), p2)
    q1, q2 = zrecv[0, 2].astype(F32), zrecv[1, 2].astype(F32)
    dout[2, pl.ds(0, hp)] += jnp.where(ld, q1, swap(q2))
    dout[2, pl.ds(hp, hp)] += jnp.where(ld, swap(q1), q2)
    for i, out in enumerate((dg, du, dd)):
        c = pltpu.make_async_copy(dout.at[i], out, out_sem.at[2 + i])
        c.start()
        outs.append(c)
    for c in made:
        c.wait_send()
    for c in outs:
        c.wait()


def hand_on(*refs):
    n = (len(refs) - 1) // 2
    cs = [pltpu.make_async_copy(refs[i], refs[n + i], refs[-1].at[i]) for i in range(n)]
    for c in cs:
        c.start()
    for c in cs:
        c.wait()


def local(tokens, expert_ids, gate_scores, gate_weight, up_weight, down_weight, grad_out):
    rows, width = tokens.shape
    _, part, hidden = gate_weight.shape
    top = expert_ids.shape[1]
    experts = lax.axis_size("expert")
    all_rows, half, hp = NY * rows, rows // 2, part // 2
    vmem, hbm = pl.BlockSpec(memory_space=pltpu.VMEM), pl.BlockSpec(memory_space=pl.ANY)
    shape = jax.ShapeDtypeStruct
    v = pltpu.VMEM
    scratch = [
        v((all_rows, width), BF16),
        v((all_rows, width), BF16),
        v((NY, experts, rows), F32),
        v((2, all_rows, hidden), F32),
        v((3, width, hidden), BF16),
        v((2, 3, hp, hidden), BF16),
        v((2, width, hidden), BF16),
        v((2, width // 2, hidden), BF16),
        v((width, hidden), BF16),
        v((all_rows, 2 * hidden), F32),
        v((all_rows, hidden), F32),
        v((all_rows, hidden), F32),
        v((2, all_rows, 2 * hidden), BF16),
        v((2, all_rows, hidden), BF16),
        v((2, all_rows, hidden), BF16),
        v((2, all_rows, hidden), BF16),
        v((NY, experts, rows), F32),
        v((NY - 1, experts, rows), F32),
        v((NX, 3, part, hidden), BF16),
        v((NX - 1, 3, part, hidden), BF16),
        v((2, NX, 3, hp, hidden), BF16),
        v((2, NX - 1, 3, hp, hidden), BF16),
        v((2, 3, hp, hidden), BF16),
        v((2, 3, hp, hidden), BF16),
        v((all_rows, width), BF16),
        v((all_rows, width), BF16),
        v((2, 2, half, width), BF16),
        v((2, rows, width), BF16),
        v((2, rows, width), BF16),
        v((3, part, hidden), F32),
        pltpu.SemaphoreType.DMA((N_COPIES,)),
        pltpu.SemaphoreType.DMA((N_COPIES,)),
        pltpu.SemaphoreType.DMA((5,)),
        pltpu.SemaphoreType.DMA((5,)),
    ]
    big, weight = shape((rows, width), BF16), shape((part, hidden), F32)
    shapes = [big, big, shape((top, rows), F32), weight, weight, weight]
    outs = pl.pallas_call(
        kernel,
        out_shape=shapes,
        in_specs=[hbm, hbm, vmem, vmem, hbm, hbm, hbm],
        out_specs=[hbm, hbm, vmem, hbm, hbm, hbm],
        scratch_shapes=scratch,
        compiler_params=pltpu.CompilerParams(
            collective_id=0, has_side_effects=True, vmem_limit_bytes=60 << 20
        ),
    )(tokens, grad_out, expert_ids.T, gate_scores.T, gate_weight[0], up_weight[0], down_weight[0])
    lo, gt, gs, dg, du, dd = pl.pallas_call(
        hand_on,
        out_shape=shapes,
        in_specs=[hbm] * 6,
        out_specs=[hbm] * 6,
        scratch_shapes=[pltpu.SemaphoreType.DMA((6,))],
    )(*outs)
    return lo, gt, gs.T, dg[None], du[None], dd[None]


def solution(mesh):
    rows_p = P(("section", "expert", "dp"), None)
    weight_p = P(("section", "expert"), "dp", None)
    return jax.shard_map(
        local,
        mesh=mesh,
        in_specs=(rows_p, rows_p, rows_p, weight_p, weight_p, weight_p, rows_p),
        out_specs=(rows_p, rows_p, rows_p, weight_p, weight_p, weight_p),
        check_vma=False,
    )
```

time: 206 us -> 244 us (1.18)
  Pallas kernels: 195 us -> 243 us
  local copies, waits for them, and re-layouts: 10 us -> 0 us
    pallas_call x1 -> x2, Pallas kernels: 195 us -> 243 us  [the longest x1 159 us: local(): pl.pallas_call(kernel, out_shape=shapes, in_specs=[hbm, hbm, vmem, vmem,...]
    unnamed x20 -> x0, local copies, waits for them, and re-layouts: 10 us -> none
where the time goes in v2:
time: 244 us
  Pallas kernels  243 us (100%)
    pallas_call x1, Pallas kernels, local(): pl.pallas_call(kernel, out_shape=shapes, in_specs=[hbm, hbm, vmem, vmem,...  159 us
    pallas_call x1, Pallas kernels, local(): pl.pallas_call(hand_on, out_shape=shapes, in_specs=[hbm] * 6, out_specs=[...  84.6 us

profile of v2, /device:TPU:1, one launch (start us, length us, event | category | flops | bytes accessed | tf_op | source)
XLA Modules:
  0.0 244.3 jit_solution(9858576167137522630)
XLA Ops:
  0.6 158.9 %shard_map.118 = (bf16[128,3072]{1,0:T(8,128)(2,1)}, bf16[128,3072]{1,0:T(8,128)(2,1)}, f32[2,128]{1,0:T(2,128)}, f32[768,128]{1,0:T(8,128)}, f32[768,128]{1,0:T(8,128)}, /*index=5*/f32[768,128]{1,0:T(8,128)}) custom-call(bf16[128,3072]{1,0:T(8,128)(2,1)} %tok.1, bf16[128,3072]{1,0:T(8,128)(2,1)} %go.1, s32[2,128]{1,0:T(2,128)} %bitcast.12, ...), custom_call_target="tpu_custom_call" | custom-call | tf_op jit(solution)/shard_map/pallas_call | solution.py:405
  159.5 84.6 %shard_map.119 = (bf16[128,3072]{1,0:T(8,128)(2,1)}, bf16[128,3072]{1,0:T(8,128)(2,1)}, f32[2,128]{1,0:T(2,128)}, f32[768,128]{1,0:T(8,128)}, f32[768,128]{1,0:T(8,128)}, /*index=5*/f32[768,128]{1,0:T(8,128)}) custom-call(bf16[128,3072]{1,0:T(8,128)(2,1)} %get-tuple-element.18.refs_0_, bf16[128,3072]{1,0:T(8,128)(2,1)} %get-tuple-element.19.refs_1_, ...), custom_call_target="tpu_custom_call" | custom-call | tf_op jit(solution)/shard_map/pallas_call | solution.py:415

commit v3 on v2

--- a/solution.py
+++ b/solution.py
@@ -347,11 +347,16 @@
 
 
 def hand_on(*refs):
-    n = (len(refs) - 1) // 2
-    cs = [pltpu.make_async_copy(refs[i], refs[n + i], refs[-1].at[i]) for i in range(n)]
-    for c in cs:
+    n = (len(refs) - 2) // 3
+    held, sem = refs[2 * n : 3 * n], refs[-2:]
+    into = [pltpu.make_async_copy(refs[i], held[i], sem[0].at[i]) for i in range(n)]
+    out = [pltpu.make_async_copy(held[i], refs[n + i], sem[1].at[i]) for i in range(n)]
+    for c in into:
         c.start()
-    for c in cs:
+    for i in range(n):
+        into[i].wait()
+        out[i].start()
+    for c in out:
         c.wait()
 
 
@@ -417,7 +422,7 @@
         out_shape=shapes,
         in_specs=[hbm] * 6,
         out_specs=[hbm] * 6,
-        scratch_shapes=[pltpu.SemaphoreType.DMA((6,))],
+        scratch_shapes=[v(o.shape, o.dtype) for o in shapes] + [pltpu.SemaphoreType.DMA((6,))] * 2,
     )(*outs)
     return lo, gt, gs.T, dg[None], du[None], dd[None]
 

time: 244 us -> 163 us (0.67)
  Pallas kernels: 243 us -> 162 us
    pallas_call x1, Pallas kernels: 84.6 us -> 2.77 us  [local(): pl.pallas_call(hand_on, out_shape=shapes, in_specs=[hbm] * 6, out_specs=[...]
where the time goes in v3:
time: 163 us; the launch traced here: 162 us
  Pallas kernels  162 us (99%)
    pallas_call x1, Pallas kernels, local(): pl.pallas_call(kernel, out_shape=shapes, in_specs=[hbm, hbm, vmem, vmem,...  159 us

profile of v3, /device:TPU:1, one launch (start us, length us, event | category | flops | bytes accessed | tf_op | source)
XLA Modules:
  0.0 162.5 jit_solution(1169021590084623157)
XLA Ops:
  0.6 158.9 %shard_map.118 = (bf16[128,3072]{1,0:T(8,128)(2,1)}, bf16[128,3072]{1,0:T(8,128)(2,1)}, f32[2,128]{1,0:T(2,128)}, f32[768,128]{1,0:T(8,128)}, f32[768,128]{1,0:T(8,128)}, /*index=5*/f32[768,128]{1,0:T(8,128)}) custom-call(bf16[128,3072]{1,0:T(8,128)(2,1)} %tok.1, bf16[128,3072]{1,0:T(8,128)(2,1)} %go.1, s32[2,128]{1,0:T(2,128)} %bitcast.12, ...), custom_call_target="tpu_custom_call" | custom-call | tf_op jit(solution)/shard_map/pallas_call | solution.py:410
  159.5 2.8 %shard_map.119 = (bf16[128,3072]{1,0:T(8,128)(2,1)}, bf16[128,3072]{1,0:T(8,128)(2,1)}, f32[2,128]{1,0:T(2,128)}, f32[768,128]{1,0:T(8,128)}, f32[768,128]{1,0:T(8,128)}, /*index=5*/f32[768,128]{1,0:T(8,128)}) custom-call(bf16[128,3072]{1,0:T(8,128)(2,1)} %get-tuple-element.18.refs_0_, bf16[128,3072]{1,0:T(8,128)(2,1)} %get-tuple-element.19.refs_1_, ...), custom_call_target="tpu_custom_call" | custom-call | tf_op jit(solution)/shard_map/pallas_call | solution.py:420

commit v4 on v3

--- a/solution.py
+++ b/solution.py
@@ -10,7 +10,7 @@
 BF16 = jnp.bfloat16
 NY = 4
 NX = 4
-N_COPIES = 128
+N_COPIES = 192
 
 
 def dot(a, b):
@@ -38,12 +38,12 @@
     lo, gt, gs, dg, du, dd,
     tokb, gob, tab, sbc, wb, pk, rw, rd, rdn,
     pre, act, act2, gub, hsb, hdup, guh, gst, gsr,
-    dwb, dwr, dwq, dwqr, zsend, zrecv, lop, gtp, far, lor, gtr, dout,
+    dwb, dwr, farw, dwq, dwqr, farq, zsend, zrecv, lop, gtp, far, lor, gtr, dout,
     send, recv, local_sem, out_sem,
 ):
     rows, width = tok.shape
     part, hidden = wg.shape
-    half, hp = rows // 2, part // 2
+    half, hp, hq = rows // 2, part // 2, part // 4
     sec, ei, x = lax.axis_index("section"), lax.axis_index("expert"), lax.axis_index("dp")
     y, zh = ei // 2, ei % 2
     other = y * 2 + 1 - zh
@@ -78,7 +78,7 @@
     def slot(j):
         return pl.ds(j * rows, rows)
 
-    mine, mine_d = x_rows(0, part), x_rows(0, hp)
+    mine = x_rows(0, part)
     w_in = (wg, wu, wd)
     own_w = [pltpu.make_async_copy(w_in[i], wb.at[i, mine], local_sem.at[i]) for i in range(3)]
     own_t = [pltpu.make_async_copy(tok, tokb.at[slot(0)], local_sem.at[3]),
@@ -107,13 +107,14 @@
 
     pl.semaphore_wait(barrier, len(peers))
 
-    def unit(h, c):
+    def unit(h, c, d=0, r0=0, size=hp):
+        at = (x + d) % NX
         if c == 2:
-            return rd.at[h, mine_d]
-        return rw.at[h, pl.ds(pl.multiple_of(x * part + c * hp, hp), hp)]
+            return rd.at[h, pl.ds(pl.multiple_of(at * hp + r0, hq), size)]
+        return rw.at[h, pl.ds(pl.multiple_of(at * part + c * hp + r0, hq), size)]
 
     units = [(h, c) for h in range(2) for c in range(3)]
-    z_w = [copy(pk.at[h, c], unit(h, c), z_peer) for h, c in units]
+    z_w = [copy(pk.at[h, c], unit(h, c), z_peer) for h, c in units[:3]]
     y_s = [copy(tab.at[0], tab.at[NY - d], y_peer(d)) for d in (2, 1, 3)]
     bufs = ((tok, tokb), (go, gob))
     y_a, y_b = [], []
@@ -123,7 +124,19 @@
                 r0 = 0 if (d == 1) == first else half
                 c = copy(src.at[pl.ds(r0, half)], dst.at[pl.ds((NY - d) * rows + r0, half)], y_peer(d))
                 (y_a if first else y_b).append(c)
-    x_w = [copy(w_in[i], wb.at[i, mine], x_peer(d)) for i in range(3) for d in (2, 1, 3)]
+    x_a, x_w = [], []
+    for first in (True, False):
+        for i in range(3):
+            for d in (1, 3):
+                r0 = 0 if (d == 1) == first else hp
+                at = pl.ds(pl.multiple_of(x * part + r0, hp), hp)
+                c = copy(w_in[i].at[pl.ds(r0, hp)], wb.at[i, at], x_peer(d))
+                (x_a if first else x_w).append(c)
+    for i in range(3):
+        for m, d in enumerate((1, 3)):
+            x_a[2 * i + m].wait_recv()
+            at = wb.at[i, pl.ds(pl.multiple_of(((x + NX - d) % NX) * part + m * hp, hp), hp)]
+            x_w.append(copy(at, at, x_peer(d)))
 
     y_c = []
     for n, (_, dst) in enumerate(bufs):
@@ -133,23 +146,32 @@
             c = copy(dst.at[pl.ds((NY - d) * rows + r0, half)], dst.at[pl.ds(2 * rows + r0, half)], y_peer(d))
             y_c.append(c)
 
-    x_r = [[], []]
+    x_n, x_r = [[] for _ in units], [[], []]
 
     def pass_on(n):
-        h, c = units[n]
         z_w[n].wait_recv()
-        for d in (2, 1, 3):
-            x_r[h].append(copy(unit(h, c), unit(h, c), x_peer(d)))
+        for d in (1, 3):
+            x_n[n].append(copy(unit(*units[n]), unit(*units[n]), x_peer(d)))
+
+    def pass_far(n):
+        for m, d in enumerate((1, 3)):
+            x_n[n][m].wait_recv()
+            at = unit(*units[n], NX - d, m * hq, hq)
+            x_r[units[n][0]].append(copy(at, at, x_peer(d)))
 
     pass_on(0)
+    pass_on(1)
+    z_w += [copy(pk.at[h, c], unit(h, c), z_peer) for h, c in units[3:]]
     for c in y_s:
         c.wait_recv()
     for r, e in ((0, ei), (1, other)):
         for j in range(NY):
             row = jnp.sum(jnp.where(sub == e, tab[j], 0.0), axis=0, keepdims=True)
             sbc[r, slot(j)] = jnp.broadcast_to(row, (rows, hidden)).T
-    for n in (1, 2, 3):
-        pass_on(n)
+    pass_far(0)
+    pass_on(2)
+    pass_far(1)
+    pass_far(2)
     for c in own_t:
         c.wait()
     for c in y_b + y_c:
@@ -216,8 +238,28 @@
 
         lax.fori_loop(0, NY, step, 0)
 
+    def halves_out(src, far_at, got, d):
+        if d == 2:
+            return [copy(src.at[pl.ds(m * far_at.shape[1], far_at.shape[1])], far_at.at[m], x_peer(e))
+                    for m, e in enumerate((1, 3))]
+        m = 0 if d == 1 else 1
+        n = far_at.shape[1]
+        return [copy(src.at[pl.ds(n - m * n, n)], got.at[m, pl.ds(n - m * n, n)], x_peer(d))]
+
+    def halves_on(src_of, far_at, got, waits):
+        n = far_at.shape[1]
+        cs = []
+        for m, d in enumerate((1, 3)):
+            waits[m].wait_recv()
+            at = pl.ds(m * n, n)
+            src = src_of(d)
+            src[at] = (src[at].astype(F32) + far_at[m].astype(F32)).astype(BF16)
+            cs.append(copy(src.at[at], got.at[m, at], x_peer(d)))
+        return cs
+
+    x_far, x_d1 = [[], []], [[[], [], []], [[], [], []]]
+
     def grads_other(h):
-        cs = [[], [], []]
         for d in (2, 1, 3, 0):
             at = x_rows(d, part)
             gu = dot_l(tokb[:, at], guh[h]).astype(BF16)
@@ -226,34 +268,40 @@
             dwq[h, d, 2] = jnp.where(ld, dn[:hp], dn[hp:]).astype(BF16)
             if d:
                 for c in range(3):
-                    cs[c].append(copy(dwq.at[h, d, c], dwqr.at[h, NX - d - 1, c], x_peer(d)))
-        return cs
-
-    def send_z(h, c, arrivals):
-        for a in arrivals:
+                    cs = halves_out(dwq.at[h, d, c], farq.at[h, c], dwqr.at[h, c], d)
+                    if d == 2:
+                        x_far[h].append(cs)
+                    else:
+                        x_d1[h][c] += cs
+
+    def grads_on(h):
+        for c in range(3):
+            x_d1[h][c] += halves_on(lambda d: dwq.at[h, d, c], farq.at[h, c], dwqr.at[h, c], x_far[h][c])
+
+    def send_z(h, c):
+        for a in x_d1[h][c]:
             a.wait_recv()
-        total = dwq[h, 0, c].astype(F32)
-        for n in range(NX - 1):
-            total += dwqr[h, n, c].astype(F32)
+        total = dwq[h, 0, c].astype(F32) + dwqr[h, c, 0].astype(F32) + dwqr[h, c, 1].astype(F32)
         zsend[h, c] = total.astype(BF16)
         return copy(zsend.at[h, c], zrecv.at[h, c], z_peer)
 
     for c in x_r[0]:
         c.wait_recv()
+    for n in (3, 4, 5):
+        pass_on(n)
     hidden_other(0)
-    x_d1 = [grads_other(0), None]
-    pass_on(4)
+    for n in (3, 4, 5):
+        pass_far(n)
+    grads_other(0)
     for c in x_w:
         c.wait_recv()
     hidden_own()
-    z_d = [send_z(0, 0, x_d1[0][0])]
-    pass_on(5)
-    for c in (1, 2):
-        z_d.append(send_z(0, c, x_d1[0][c]))
+    grads_on(0)
 
     for c in x_r[1]:
         c.wait_recv()
     hidden_other(1)
+    z_d = [send_z(0, c) for c in range(3)]
     lall = low((hp, hidden))
     for s in range(NX):
         d0, d1 = rd[0, pl.ds(s * hp, hp)].astype(F32), rd[1, pl.ds(s * hp, hp)].astype(F32)
@@ -281,47 +329,55 @@
         for m, d in enumerate((1, 3)):
             r0 = half - m * half
             y_o.append(copy(buf.at[pl.ds(d * rows + r0, half)], dst.at[m, pl.ds(r0, half)], y_peer(d)))
-    x_d1[1] = grads_other(1)
-    k = 0
+    grads_other(1)
+
+    w_far, x_d0 = [], []
+    for d in (2, 1, 3, 0):
+        at = x_rows(d, part)
+        both = dot_l(tokb[:, at], gub[0]).astype(BF16)
+        dwb[d, 0], dwb[d, 1] = both[:, :hidden], both[:, hidden:]
+        dwb[d, 2] = dot_l(gob[:, at], hsb[0]).astype(BF16)
+        if d == 2:
+            grads_on(1)
+        if d:
+            for i in range(3):
+                cs = halves_out(dwb.at[d, i], farw.at[i], dwr.at[i], d)
+                if d == 2:
+                    w_far.append(cs)
+                else:
+                    x_d0 += cs
+
     for s in range(NX):
         cols = pl.ds(s * part, part)
         for n, (buf, dst) in enumerate(((lop, lor), (gtp, gtr))):
             for m, d in enumerate((1, 3)):
                 r0 = m * half
-                y_far[k].wait_recv()
-                k += 1
+                y_far[4 * s + 2 * n + m].wait_recv()
                 at = pl.ds(d * rows + r0, half)
                 buf[at, cols] = (buf[at, cols].astype(F32) + far[n, m, :, cols].astype(F32)).astype(BF16)
                 y_o.append(copy(buf.at[at, cols], dst.at[m, pl.ds(r0, half), cols], y_peer(d)))
-        if s < 3:
-            z_d.append(send_z(1, s, x_d1[1][s]))
-
-    x_d0 = []
-    for d in (2, 1, 3, 0):
-        at = x_rows(d, part)
-        both = dot_l(tokb[:, at], gub[0]).astype(BF16)
-        dwb[d, 0], dwb[d, 1] = both[:, :hidden], both[:, hidden:]
-        dwb[d, 2] = dot_l(gob[:, at], hsb[0]).astype(BF16)
-        if d:
-            for i in range(3):
-                x_d0.append(copy(dwb.at[d, i], dwr.at[NX - d - 1, i], x_peer(d)))
+        if s == 2:
+            z_d += [send_z(1, c) for c in range(3)]
+    for i in range(3):
+        x_d0 += halves_on(lambda d: dwb.at[d, i], farw.at[i], dwr.at[i], w_far[i])
     for c in x_d0:
         c.wait_recv()
     for i in range(3):
-        total = dwb[0, i].astype(F32)
-        for n in range(NX - 1):
-            total += dwr[n, i].astype(F32)
-        dout[i] = total
+        dout[i] = dwb[0, i].astype(F32) + dwr[i, 0].astype(F32) + dwr[i, 1].astype(F32)
 
     outs = []
-    for c in y_g + y_o:
-        c.wait_recv()
-    for n, (buf, got, out) in enumerate(((lop, lor, lo), (gtp, gtr, gt))):
-        total = buf[slot(0)].astype(F32) + got[0].astype(F32) + got[1].astype(F32)
-        buf[slot(0)] = total.astype(BF16)
-        c = pltpu.make_async_copy(buf.at[slot(0)], out, out_sem.at[n])
-        c.start()
-        outs.append(c)
+    for c in y_g + y_o[:4]:
+        c.wait_recv()
+    for s in range(NX):
+        cols = pl.ds(s * part, part)
+        for n, (buf, got, out) in enumerate(((lop, lor, lo), (gtp, gtr, gt))):
+            for m in range(2):
+                y_o[4 + 4 * s + 2 * n + m].wait_recv()
+            total = buf[slot(0), cols].astype(F32) + got[0, :, cols].astype(F32) + got[1, :, cols].astype(F32)
+            buf[slot(0), cols] = total.astype(BF16)
+            c = pltpu.make_async_copy(buf.at[slot(0), cols], out.at[:, cols], out_sem.at[2 * s + n])
+            c.start()
+            outs.append(c)
     gs_sum = gst[0] + gsr[0] + gsr[1] + gsr[2]
     for k in range(ids.shape[0]):
         gs[k : k + 1] = jnp.sum(jnp.where(sub == ids[k : k + 1], gs_sum, 0.0), axis=0, keepdims=True)
@@ -337,7 +393,7 @@
     dout[2, pl.ds(0, hp)] += jnp.where(ld, q1, swap(q2))
     dout[2, pl.ds(hp, hp)] += jnp.where(ld, swap(q1), q2)
     for i, out in enumerate((dg, du, dd)):
-        c = pltpu.make_async_copy(dout.at[i], out, out_sem.at[2 + i])
+        c = pltpu.make_async_copy(dout.at[i], out, out_sem.at[2 * NX + i])
         c.start()
         outs.append(c)
     for c in made:
@@ -389,9 +445,11 @@
         v((NY, experts, rows), F32),
         v((NY - 1, experts, rows), F32),
         v((NX, 3, part, hidden), BF16),
-        v((NX - 1, 3, part, hidden), BF16),
+        v((3, 2, part, hidden), BF16),
+        v((3, 2, hp, hidden), BF16),
         v((2, NX, 3, hp, hidden), BF16),
-        v((2, NX - 1, 3, hp, hidden), BF16),
+        v((2, 3, 2, hp, hidden), BF16),
+        v((2, 3, 2, hp // 2, hidden), BF16),
         v((2, 3, hp, hidden), BF16),
         v((2, 3, hp, hidden), BF16),
         v((all_rows, width), BF16),
@@ -403,7 +461,7 @@
         pltpu.SemaphoreType.DMA((N_COPIES,)),
         pltpu.SemaphoreType.DMA((N_COPIES,)),
         pltpu.SemaphoreType.DMA((5,)),
-        pltpu.SemaphoreType.DMA((5,)),
+        pltpu.SemaphoreType.DMA((2 * NX + 3,)),
     ]
     big, weight = shape((rows, width), BF16), shape((part, hidden), F32)
     shapes = [big, big, shape((top, rows), F32), weight, weight, weight]

time: 163 us -> 151 us (0.926)
  Pallas kernels: 162 us -> 149 us
    pallas_call x1, Pallas kernels: 159 us -> 146 us  [local(): pl.pallas_call(kernel, out_shape=shapes, in_specs=[hbm, hbm, vmem, vmem,...]
where the time goes in v4:
time: 151 us; the launch traced here: 150 us
  Pallas kernels  149 us (99%)
    pallas_call x1, Pallas kernels, local(): pl.pallas_call(kernel, out_shape=shapes, in_specs=[hbm, hbm, vmem, vmem,...  146 us

profile of v4, /device:TPU:1, one launch (start us, length us, event | category | flops | bytes accessed | tf_op | source)
XLA Modules:
  0.0 150.0 jit_solution(12643000342356137504)
XLA Ops:
  0.6 146.5 %shard_map.118 = (bf16[128,3072]{1,0:T(8,128)(2,1)}, bf16[128,3072]{1,0:T(8,128)(2,1)}, f32[2,128]{1,0:T(2,128)}, f32[768,128]{1,0:T(8,128)}, f32[768,128]{1,0:T(8,128)}, /*index=5*/f32[768,128]{1,0:T(8,128)}) custom-call(bf16[128,3072]{1,0:T(8,128)(2,1)} %tok.1, bf16[128,3072]{1,0:T(8,128)(2,1)} %go.1, s32[2,128]{1,0:T(2,128)} %bitcast.12, ...), custom_call_target="tpu_custom_call" | custom-call | tf_op jit(solution)/shard_map/pallas_call | solution.py:468
  147.1 2.8 %shard_map.119 = (bf16[128,3072]{1,0:T(8,128)(2,1)}, bf16[128,3072]{1,0:T(8,128)(2,1)}, f32[2,128]{1,0:T(2,128)}, f32[768,128]{1,0:T(8,128)}, f32[768,128]{1,0:T(8,128)}, /*index=5*/f32[768,128]{1,0:T(8,128)}) custom-call(bf16[128,3072]{1,0:T(8,128)(2,1)} %get-tuple-element.18.refs_0_, bf16[128,3072]{1,0:T(8,128)(2,1)} %get-tuple-element.19.refs_1_, ...), custom_call_target="tpu_custom_call" | custom-call | tf_op jit(solution)/shard_map/pallas_call | solution.py:478

commit v5 on v4

--- a/solution.py
+++ b/solution.py
@@ -11,6 +11,8 @@
 NY = 4
 NX = 4
 N_COPIES = 192
+FIRST = 5
+PLACE = (0, 1, 3, 2)
 
 
 def dot(a, b):
@@ -75,8 +77,8 @@
     def x_rows(d, size):
         return pl.ds(pl.multiple_of(((x + d) % NX) * size, size), size)
 
-    def slot(j):
-        return pl.ds(j * rows, rows)
+    def slot(j, r0=0, size=rows):
+        return pl.ds(PLACE[j] * rows + r0, size)
 
     mine = x_rows(0, part)
     w_in = (wg, wu, wd)
@@ -114,15 +116,15 @@
         return rw.at[h, pl.ds(pl.multiple_of(at * part + c * hp + r0, hq), size)]
 
     units = [(h, c) for h in range(2) for c in range(3)]
-    z_w = [copy(pk.at[h, c], unit(h, c), z_peer) for h, c in units[:3]]
-    y_s = [copy(tab.at[0], tab.at[NY - d], y_peer(d)) for d in (2, 1, 3)]
+    z_w = [copy(pk.at[h, c], unit(h, c), z_peer) for h, c in units[:FIRST]]
+    y_s = [copy(tab.at[0], tab.at[PLACE[NY - d]], y_peer(d)) for d in (2, 1, 3)]
     bufs = ((tok, tokb), (go, gob))
     y_a, y_b = [], []
     for first in (True, False):
         for src, dst in bufs:
             for d in (1, 3):
                 r0 = 0 if (d == 1) == first else half
-                c = copy(src.at[pl.ds(r0, half)], dst.at[pl.ds((NY - d) * rows + r0, half)], y_peer(d))
+                c = copy(src.at[pl.ds(r0, half)], dst.at[slot(NY - d, r0, half)], y_peer(d))
                 (y_a if first else y_b).append(c)
     x_a, x_w = [], []
     for first in (True, False):
@@ -143,7 +145,7 @@
         for m, d in enumerate((1, 3)):
             y_a[2 * n + m].wait_recv()
             r0 = 0 if d == 1 else half
-            c = copy(dst.at[pl.ds((NY - d) * rows + r0, half)], dst.at[pl.ds(2 * rows + r0, half)], y_peer(d))
+            c = copy(dst.at[slot(NY - d, r0, half)], dst.at[slot(2, r0, half)], y_peer(d))
             y_c.append(c)
 
     x_n, x_r = [[] for _ in units], [[], []]
@@ -161,20 +163,22 @@
 
     pass_on(0)
     pass_on(1)
-    z_w += [copy(pk.at[h, c], unit(h, c), z_peer) for h, c in units[3:]]
+    z_w += [copy(pk.at[h, c], unit(h, c), z_peer) for h, c in units[FIRST:]]
     for c in y_s:
         c.wait_recv()
     for r, e in ((0, ei), (1, other)):
         for j in range(NY):
             row = jnp.sum(jnp.where(sub == e, tab[j], 0.0), axis=0, keepdims=True)
-            sbc[r, slot(j)] = jnp.broadcast_to(row, (rows, hidden)).T
+            sbc[r, pl.ds(j * rows, rows)] = jnp.broadcast_to(row, (rows, hidden)).T
     pass_far(0)
     pass_on(2)
     pass_far(1)
+    pass_on(3)
     pass_far(2)
+    pass_far(3)
     for c in own_t:
         c.wait()
-    for c in y_b + y_c:
+    for c in y_b:
         c.wait_recv()
 
     def add_score(j, e, col):
@@ -184,9 +188,10 @@
     for j in range(NY):
         gst[j] = jnp.zeros(sub.shape, F32)
 
-    def hidden_own():
-        pre[...] = dot(tokb[...], jnp.concatenate([wb[0], wb[1]], axis=1))
-        act[...] = dot(gob[...], wb[2])
+    def hidden_own(j0, j1):
+        every = pl.ds(j0 * rows, (j1 - j0) * rows)
+        pre[every] = dot(tokb[every], jnp.concatenate([wb[0], wb[1]], axis=1))
+        act[every] = dot(gob[every], wb[2])
 
         def step(j, _):
             at = pl.ds(pl.multiple_of(j * rows, rows), rows)
@@ -201,21 +206,22 @@
             add_score(j, ei, jnp.sum(h * a, axis=1, keepdims=True))
             return 0
 
-        lax.fori_loop(0, NY, step, 0)
+        lax.fori_loop(j0, j1, step, 0)
 
     lr = low((rows, hidden))
 
-    def hidden_other(h):
-        pre[:, :hidden] = dot(tokb[...], rw[h])
+    def hidden_other(h, j0, j1):
+        every = pl.ds(j0 * rows, (j1 - j0) * rows)
+        pre[every, :hidden] = dot(tokb[every], rw[h])
         for s in range(NX):
             dn = rd[h, pl.ds(s * hp, hp)]
-            a1 = dot(gob[:, pl.ds(s * part, hp)], dn)
-            a2 = dot(gob[:, pl.ds(s * part + hp, hp)], dn)
+            a1 = dot(gob[every, pl.ds(s * part, hp)], dn)
+            a2 = dot(gob[every, pl.ds(s * part + hp, hp)], dn)
             if s == 0:
-                act[...], act2[...] = a1, a2
+                act[every], act2[every] = a1, a2
             else:
-                act[...] += a1
-                act2[...] += a2
+                act[every] += a1
+                act2[every] += a2
 
         def step(j, _):
             at = pl.ds(pl.multiple_of(j * rows, rows), rows)
@@ -236,7 +242,7 @@
             add_score(j, other, jnp.sum(jnp.where(lr, hid * a, 0.0), axis=1, keepdims=True))
             return 0
 
-        lax.fori_loop(0, NY, step, 0)
+        lax.fori_loop(j0, j1, step, 0)
 
     def halves_out(src, far_at, got, d):
         if d == 2:
@@ -266,17 +272,14 @@
             dn = dot_l(gob[:, at], hdup[h])
             dwq[h, d, 0], dwq[h, d, 1] = gu[:hp], gu[hp:]
             dwq[h, d, 2] = jnp.where(ld, dn[:hp], dn[hp:]).astype(BF16)
-            if d:
-                for c in range(3):
-                    cs = halves_out(dwq.at[h, d, c], farq.at[h, c], dwqr.at[h, c], d)
-                    if d == 2:
-                        x_far[h].append(cs)
-                    else:
-                        x_d1[h][c] += cs
-
-    def grads_on(h):
-        for c in range(3):
-            x_d1[h][c] += halves_on(lambda d: dwq.at[h, d, c], farq.at[h, c], dwqr.at[h, c], x_far[h][c])
+
+    def grads_out(h, c):
+        x_far[h].append(halves_out(dwq.at[h, 2, c], farq.at[h, c], dwqr.at[h, c], 2))
+        for d in (1, 3):
+            x_d1[h][c] += halves_out(dwq.at[h, d, c], farq.at[h, c], dwqr.at[h, c], d)
+
+    def grads_on(h, c):
+        x_d1[h][c] += halves_on(lambda d: dwq.at[h, d, c], farq.at[h, c], dwqr.at[h, c], x_far[h][c])
 
     def send_z(h, c):
         for a in x_d1[h][c]:
@@ -285,23 +288,32 @@
         zsend[h, c] = total.astype(BF16)
         return copy(zsend.at[h, c], zrecv.at[h, c], z_peer)
 
+    for c in x_w:
+        c.wait_recv()
+    hidden_own(0, 3)
     for c in x_r[0]:
         c.wait_recv()
-    for n in (3, 4, 5):
-        pass_on(n)
-    hidden_other(0)
-    for n in (3, 4, 5):
-        pass_far(n)
+    hidden_other(0, 0, 3)
+    for c in y_c:
+        c.wait_recv()
+    pass_on(4)
+    hidden_other(0, 3, 4)
+    pass_on(5)
+    pass_far(4)
     grads_other(0)
-    for c in x_w:
-        c.wait_recv()
-    hidden_own()
-    grads_on(0)
+    pass_far(5)
+    grads_out(0, 0)
+    hidden_own(3, 4)
+    grads_on(0, 0)
 
     for c in x_r[1]:
         c.wait_recv()
-    hidden_other(1)
-    z_d = [send_z(0, c) for c in range(3)]
+    grads_out(0, 1)
+    grads_out(0, 2)
+    hidden_other(1, 0, NY)
+    z_d = [send_z(0, 0)]
+    grads_on(0, 1)
+    grads_on(0, 2)
     lall = low((hp, hidden))
     for s in range(NX):
         d0, d1 = rd[0, pl.ds(s * hp, hp)].astype(F32), rd[1, pl.ds(s * hp, hp)].astype(F32)
@@ -321,31 +333,34 @@
         for n, buf in enumerate((lop, gtp)):
             for m, d in enumerate((1, 3)):
                 r0 = m * half
-                c = copy(buf.at[pl.ds(2 * rows + r0, half), cols], far.at[n, m, :, cols], y_peer(d))
+                c = copy(buf.at[slot(2, r0, half), cols], far.at[n, m, :, cols], y_peer(d))
                 y_far.append(c)
-    y_g = [copy(gst.at[d], gsr.at[NY - d - 1], y_peer(d)) for d in (2, 1, 3)]
+        if s in (1, 2):
+            z_d.append(send_z(0, s))
+    y_g = [copy(gst.at[PLACE[d]], gsr.at[NY - d - 1], y_peer(d)) for d in (2, 1, 3)]
     y_o = []
     for buf, dst in ((lop, lor), (gtp, gtr)):
         for m, d in enumerate((1, 3)):
             r0 = half - m * half
-            y_o.append(copy(buf.at[pl.ds(d * rows + r0, half)], dst.at[m, pl.ds(r0, half)], y_peer(d)))
+            y_o.append(copy(buf.at[slot(d, r0, half)], dst.at[m, pl.ds(r0, half)], y_peer(d)))
     grads_other(1)
-
-    w_far, x_d0 = [], []
+    for c in range(3):
+        grads_out(1, c)
+
     for d in (2, 1, 3, 0):
         at = x_rows(d, part)
         both = dot_l(tokb[:, at], gub[0]).astype(BF16)
         dwb[d, 0], dwb[d, 1] = both[:, :hidden], both[:, hidden:]
         dwb[d, 2] = dot_l(gob[:, at], hsb[0]).astype(BF16)
-        if d == 2:
-            grads_on(1)
-        if d:
-            for i in range(3):
-                cs = halves_out(dwb.at[d, i], farw.at[i], dwr.at[i], d)
-                if d == 2:
-                    w_far.append(cs)
-                else:
-                    x_d0 += cs
+    for c in range(3):
+        grads_on(1, c)
+    z_d += [send_z(1, c) for c in range(3)]
+    w_far, x_d0 = [], []
+    for i in range(3):
+        w_far.append(halves_out(dwb.at[2, i], farw.at[i], dwr.at[i], 2))
+    for i in range(3):
+        for d in (1, 3):
+            x_d0 += halves_out(dwb.at[d, i], farw.at[i], dwr.at[i], d)
 
     for s in range(NX):
         cols = pl.ds(s * part, part)
@@ -353,11 +368,9 @@
             for m, d in enumerate((1, 3)):
                 r0 = m * half
                 y_far[4 * s + 2 * n + m].wait_recv()
-                at = pl.ds(d * rows + r0, half)
+                at = slot(d, r0, half)
                 buf[at, cols] = (buf[at, cols].astype(F32) + far[n, m, :, cols].astype(F32)).astype(BF16)
                 y_o.append(copy(buf.at[at, cols], dst.at[m, pl.ds(r0, half), cols], y_peer(d)))
-        if s == 2:
-            z_d += [send_z(1, c) for c in range(3)]
     for i in range(3):
         x_d0 += halves_on(lambda d: dwb.at[d, i], farw.at[i], dwr.at[i], w_far[i])
     for c in x_d0:
@@ -382,17 +395,20 @@
     for k in range(ids.shape[0]):
         gs[k : k + 1] = jnp.sum(jnp.where(sub == ids[k : k + 1], gs_sum, 0.0), axis=0, keepdims=True)
 
-    for c in z_d:
-        c.wait_recv()
     for c in range(2):
+        z_d[c].wait_recv()
+        z_d[3 + c].wait_recv()
         at = pl.ds(c * hp, hp)
         p1, p2 = zrecv[0, c].astype(F32), zrecv[1, c].astype(F32)
         dout[0, at] += jnp.where(ld, p1, swap(p2))
         dout[1, at] += jnp.where(ld, swap(p1), p2)
-    q1, q2 = zrecv[0, 2].astype(F32), zrecv[1, 2].astype(F32)
-    dout[2, pl.ds(0, hp)] += jnp.where(ld, q1, swap(q2))
-    dout[2, pl.ds(hp, hp)] += jnp.where(ld, swap(q1), q2)
     for i, out in enumerate((dg, du, dd)):
+        if i == 2:
+            z_d[2].wait_recv()
+            z_d[5].wait_recv()
+            q1, q2 = zrecv[0, 2].astype(F32), zrecv[1, 2].astype(F32)
+            dout[2, pl.ds(0, hp)] += jnp.where(ld, q1, swap(q2))
+            dout[2, pl.ds(hp, hp)] += jnp.where(ld, swap(q1), q2)
         c = pltpu.make_async_copy(dout.at[i], out, out_sem.at[2 * NX + i])
         c.start()
         outs.append(c)

time: 151 us -> 148 us (0.980)
  the two profiles are of different devices: /device:TPU:1 before, /device:TPU:72 now
where the time goes in v5:
time: 148 us
  Pallas kernels  147 us (99%)
    pallas_call x1, Pallas kernels, local(): pl.pallas_call(kernel, out_shape=shapes, in_specs=[hbm, hbm, vmem, vmem,...  144 us

profile of v5, /device:TPU:72, one launch (start us, length us, event | category | flops | bytes accessed | tf_op | source)
XLA Modules:
  0.0 147.8 jit_solution(913789983418841624)
XLA Ops:
  0.6 144.2 %shard_map.118 = (bf16[128,3072]{1,0:T(8,128)(2,1)}, bf16[128,3072]{1,0:T(8,128)(2,1)}, f32[2,128]{1,0:T(2,128)}, f32[768,128]{1,0:T(8,128)}, f32[768,128]{1,0:T(8,128)}, /*index=5*/f32[768,128]{1,0:T(8,128)}) custom-call(bf16[128,3072]{1,0:T(8,128)(2,1)} %tok.1, bf16[128,3072]{1,0:T(8,128)(2,1)} %go.1, s32[2,128]{1,0:T(2,128)} %bitcast.12, ...), custom_call_target="tpu_custom_call" | custom-call | tf_op jit(solution)/shard_map/pallas_call | solution.py:484
  144.9 2.8 %shard_map.119 = (bf16[128,3072]{1,0:T(8,128)(2,1)}, bf16[128,3072]{1,0:T(8,128)(2,1)}, f32[2,128]{1,0:T(2,128)}, f32[768,128]{1,0:T(8,128)}, f32[768,128]{1,0:T(8,128)}, /*index=5*/f32[768,128]{1,0:T(8,128)}) custom-call(bf16[128,3072]{1,0:T(8,128)(2,1)} %get-tuple-element.18.refs_0_, bf16[128,3072]{1,0:T(8,128)(2,1)} %get-tuple-element.19.refs_1_, ...), custom_call_target="tpu_custom_call" | custom-call | tf_op jit(solution)/shard_map/pallas_call | solution.py:494

commit v6 on v5

--- a/solution.py
+++ b/solution.py
@@ -304,16 +304,14 @@
     pass_far(5)
     grads_out(0, 0)
     hidden_own(3, 4)
+
+    for c in x_r[1]:
+        c.wait_recv()
     grads_on(0, 0)
-
-    for c in x_r[1]:
-        c.wait_recv()
     grads_out(0, 1)
     grads_out(0, 2)
     hidden_other(1, 0, NY)
-    z_d = [send_z(0, 0)]
-    grads_on(0, 1)
-    grads_on(0, 2)
+    z_d = []
     lall = low((hp, hidden))
     for s in range(NX):
         d0, d1 = rd[0, pl.ds(s * hp, hp)].astype(F32), rd[1, pl.ds(s * hp, hp)].astype(F32)
@@ -335,14 +333,18 @@
                 r0 = m * half
                 c = copy(buf.at[slot(2, r0, half), cols], far.at[n, m, :, cols], y_peer(d))
                 y_far.append(c)
-        if s in (1, 2):
-            z_d.append(send_z(0, s))
+        if s == 0:
+            z_d.append(send_z(0, 0))
+        if s == 1:
+            grads_on(0, 1)
+            grads_on(0, 2)
     y_g = [copy(gst.at[PLACE[d]], gsr.at[NY - d - 1], y_peer(d)) for d in (2, 1, 3)]
     y_o = []
     for buf, dst in ((lop, lor), (gtp, gtr)):
         for m, d in enumerate((1, 3)):
             r0 = half - m * half
             y_o.append(copy(buf.at[slot(d, r0, half)], dst.at[m, pl.ds(r0, half)], y_peer(d)))
+    z_d += [send_z(0, 1), send_z(0, 2)]
     grads_other(1)
     for c in range(3):
         grads_out(1, c)
@@ -373,11 +375,6 @@
                 y_o.append(copy(buf.at[at, cols], dst.at[m, pl.ds(r0, half), cols], y_peer(d)))
     for i in range(3):
         x_d0 += halves_on(lambda d: dwb.at[d, i], farw.at[i], dwr.at[i], w_far[i])
-    for c in x_d0:
-        c.wait_recv()
-    for i in range(3):
-        dout[i] = dwb[0, i].astype(F32) + dwr[i, 0].astype(F32) + dwr[i, 1].astype(F32)
-
     outs = []
     for c in y_g + y_o[:4]:
         c.wait_recv()
@@ -395,6 +392,10 @@
     for k in range(ids.shape[0]):
         gs[k : k + 1] = jnp.sum(jnp.where(sub == ids[k : k + 1], gs_sum, 0.0), axis=0, keepdims=True)
 
+    for c in x_d0:
+        c.wait_recv()
+    for i in range(3):
+        dout[i] = dwb[0, i].astype(F32) + dwr[i, 0].astype(F32) + dwr[i, 1].astype(F32)
     for c in range(2):
         z_d[c].wait_recv()
         z_d[3 + c].wait_recv()

time: 148 us -> 147 us (level)
  the two profiles are of different devices: /device:TPU:72 before, /device:TPU:64 now
where the time goes in v6:
time: 147 us; the launch traced here: 146 us
  Pallas kernels  146 us (99%)
    pallas_call x1, Pallas kernels, local(): pl.pallas_call(kernel, out_shape=shapes, in_specs=[hbm, hbm, vmem, vmem,...  143 us

profile of v6, /device:TPU:64, one launch (start us, length us, event | category | flops | bytes accessed | tf_op | source)
XLA Modules:
  0.0 146.4 jit_solution(14489145474925728612)
XLA Ops:
  0.6 142.8 %shard_map.118 = (bf16[128,3072]{1,0:T(8,128)(2,1)}, bf16[128,3072]{1,0:T(8,128)(2,1)}, f32[2,128]{1,0:T(2,128)}, f32[768,128]{1,0:T(8,128)}, f32[768,128]{1,0:T(8,128)}, /*index=5*/f32[768,128]{1,0:T(8,128)}) custom-call(bf16[128,3072]{1,0:T(8,128)(2,1)} %tok.1, bf16[128,3072]{1,0:T(8,128)(2,1)} %go.1, s32[2,128]{1,0:T(2,128)} %bitcast.12, ...), custom_call_target="tpu_custom_call" | custom-call | tf_op jit(solution)/shard_map/pallas_call | solution.py:485
  143.5 2.8 %shard_map.119 = (bf16[128,3072]{1,0:T(8,128)(2,1)}, bf16[128,3072]{1,0:T(8,128)(2,1)}, f32[2,128]{1,0:T(2,128)}, f32[768,128]{1,0:T(8,128)}, f32[768,128]{1,0:T(8,128)}, /*index=5*/f32[768,128]{1,0:T(8,128)}) custom-call(bf16[128,3072]{1,0:T(8,128)(2,1)} %get-tuple-element.18.refs_0_, bf16[128,3072]{1,0:T(8,128)(2,1)} %get-tuple-element.19.refs_1_, ...), custom_call_target="tpu_custom_call" | custom-call | tf_op jit(solution)/shard_map/pallas_call | solution.py:495
